TPU v7x, 256 devices: a whole 4x4x8 slice. The times are simulated.
256 devices in a mesh: prow: 16 (over z, core), pcol: 16 (over y, x).
Axes of the slice: x: 4, y: 4, z: 8, core: 2. Of those that a mesh axis runs over, the one named last changes fastest.
Arguments:
- matrix: float32 [1, 8192, 1, 8192], P(None, 'prow', None, 'pcol'), may hold values from -6 to 6
- pivots: int32 [2, 512], replicated, may hold values from 1024 to 8191, as said below
- lower_inv: float32 [2, 512, 512], replicated, as said below
- upper_inv: float32 [2, 512, 512], replicated, as said below
Outputs:
- factored: float32 [1, 8192, 1, 8192], P(None, 'prow', None, 'pcol')
Inputs may be any that keep to these rules, and one draw needn't show every extreme that they name: `pivots`: in step k the 512 entries are distinct rows; at most 37 of them lie in rows held by one index of prow, and exactly 37 for some index. `lower_inv`: each of the 2 matrices is unit lower triangular. `upper_inv`: each of the 2 matrices is upper triangular with a nonzero diagonal.
All inputs are finite; a program needn't handle non-finite values.
Results may differ from a plain program's by a relative error of at most 0.0001.
Values sent between devices are 32-bit elements; how exact they have to be, the bound alone decides.
A program may use at most 64 MiB of HBM per device.

v0:
```python
import jax
import jax.numpy as jnp
from jax import lax
from jax.sharding import PartitionSpec as P


def spread(value, axis, source):
    kept = jnp.where(lax.axis_index(axis) == source, value, 0).astype(value.dtype)
    return lax.psum(kept, axis)


def body(matrix, pivots, lower_inv, upper_inv):
    blk_rows, row_width, blk_cols, col_width = matrix.shape
    n_prow = lax.axis_size("prow")
    n_pcol = lax.axis_size("pcol")
    prow_index = lax.axis_index("prow")
    pcol_index = lax.axis_index("pcol")
    step_count = pivots.shape[0]
    highest = lax.Precision.HIGHEST
    tile_data = matrix.reshape(blk_rows * row_width, blk_cols * row_width)
    row_ids = (
        (jnp.arange(blk_rows)[:, None] * n_prow + prow_index) * row_width
        + jnp.arange(row_width)[None, :]
    ).reshape(-1)
    col_ids = (
        (jnp.arange(blk_cols)[:, None] * n_pcol + pcol_index) * row_width
        + jnp.arange(row_width)[None, :]
    ).reshape(-1)
    slot_numbers = jnp.arange(row_width)
    for step in range(step_count):
        start = step * row_width
        chosen = pivots[step]
        chosen_block = chosen // row_width
        owner_row = chosen_block % n_prow
        owned_here = owner_row == prow_index
        local_rows = chosen_block // n_prow * row_width + chosen % row_width
        picked = jnp.take(tile_data, jnp.where(owned_here, local_rows, 0), axis=0)
        picked = jnp.where(owned_here[:, None], picked, 0.0)
        matches = row_ids[:, None] == chosen[None, :]
        is_target = jnp.any(matches, axis=1)
        slot_index = jnp.sum(jnp.where(matches, slot_numbers[None, :], 0), axis=1)
        old_rows = spread(tile_data, "prow", step)
        tile_data = jnp.where(is_target[:, None], jnp.take(old_rows, slot_index, axis=0), tile_data)
        trailing = col_ids >= start + row_width
        new_row = lax.psum(picked, "prow")
        applied = jnp.dot(lower_inv[step], new_row, precision=highest)
        final_row = jnp.where(trailing[None, :], applied, new_row)
        head_here = prow_index == step
        tile_data = tile_data.at[0:row_width].set(jnp.where(head_here, final_row, tile_data))
        below_rows = row_ids >= start + row_width
        panel_cols = tile_data
        multiplied = jnp.dot(panel_cols, upper_inv[step], precision=highest)
        lower_here = jnp.where(below_rows[:, None], multiplied, 0.0)
        lower_part = spread(lower_here, "pcol", step)
        panel_here = jnp.logical_and(pcol_index == step, below_rows[:, None])
        tile_data = tile_data.at[:, 0:row_width].set(jnp.where(panel_here, lower_part, panel_cols))
        upper_part = jnp.where(trailing[None, :], final_row, 0.0)
        tile_data = tile_data - jnp.dot(lower_part, upper_part, precision=highest)
    return tile_data.reshape(matrix.shape)


def solution(mesh):
    placed = (P(None, "prow", None, "pcol"), P(), P(), P())
    return jax.shard_map(
        body, mesh=mesh, in_specs=placed, out_specs=P(None, "prow", None, "pcol"), check_vma=False
    )
```

profile of v0, /device:TPU:39, one launch (start us, length us, event | category | flops | bytes accessed | tf_op | source)
XLA Modules:
  0.0 484.8 jit_solution(2150133056130299124)
XLA Ops:
  6.5 0.0 copy-start.1
  6.5 0.0 all-reduce.13.cloned.1.call-start
  6.5 0.0 copy-start.5
  6.5 1.4 copy.39
  7.9 0.1 copy-done.1
  8.1 1.3 copy.19
  9.4 0.0 copy-done.5
  9.5 1.6 gather_fusion
  11.1 0.3 copy.21
  11.4 1.6 bitcast_select_fusion
  13.1 0.0 all-reduce.13.cloned.1.call-update
  13.1 0.0 all-reduce.7.cloned.1.call-start
  13.2 0.4 fusion.6
  13.6 0.4 compare_reduce_fusion
  14.0 114.4 %all-reduce.13.cloned.1.call-done = (f32[512,512]{0,1:T(8,128)}, f32[512,512]{0,1:T(8,128)}) async-done(((f32[512,512]{0,1:T(8,128)}, f32[512,512]{0,1:T(8,128)}), (f32[512,512]{0,1:T(8,128)}, f32[512,512]{0,1:T(8,128)})) %all-reduce.13.cloned.1.call-update) | async-done | bytes 2097168 | tf_op jit(solution)/shard_map/psum | solution.py:45
  128.3 1.6 copy.22
  129.9 2.3 gather_fusion.1
  132.2 0.0 copy-start.4
  132.2 1.6 copy.23
  133.9 0.0 copy-start.2
  133.9 0.0 copy-done.4
  133.9 3.3 fusion.2
  137.3 0.0 copy-start
  137.3 1.0 copy-done
  138.3 0.0 copy-done.2
  138.3 3.0 fusion.4
  141.3 0.0 all-reduce.7.cloned.1.call-update
  141.3 0.0 all-reduce.11.cloned.1.call-start
  141.5 97.3 %all-reduce.7.cloned.1.call-done = f32[512,512]{0,1:T(8,128)} async-done(((f32[512,512]{0,1:T(8,128)}), f32[512,512]{0,1:T(8,128)}) %all-reduce.7.cloned.1.call-update) | async-done | bytes 1048592 | tf_op jit(solution)/shard_map/psum | solution.py:9
  238.8 5.2 %broadcast_select_fusion = (f32[512,512]{0,1:T(8,128)}, f32[512,512]{0,1:T(8,128)S(1)}) fusion(pred[]{:T(512)S(6)} %eq.64, f32[512,512]{0,1:T(8,128)} %all-reduce.7.cloned.1.call-done, f32[512,512]{0,1:T(8,128)} %copy-done, pred[512]{0:T(512)(128)(4,1)S(1)} %fusion.33, f32[1,512,1,512]{1,3,2,0:T(8,128)S(1)} %copy.19, f32[512,512]{0,1:T(8,128)S(1)} %copy.23, ...), kind=kOutput, calls=%fused_computation.40 | convolution fusion | flops 1612447744 | bytes 6293506 | tf_op jit(solution)/shard_map/dot_general | solution.py:58
  244.0 0.3 copy.26
  244.3 1.6 gather_fusion.2
  245.9 0.3 copy.27
  246.3 1.1 select_select_fusion.1
  247.4 0.0 all-reduce.11.cloned.1.call-update
  247.4 0.2 all-reduce.9.cloned.1.call-start
  247.7 114.5 %all-reduce.11.cloned.1.call-done = (f32[512,512]{0,1:T(8,128)}, f32[512,512]{0,1:T(8,128)}) async-done(((f32[512,512]{0,1:T(8,128)}, f32[512,512]{0,1:T(8,128)}), (f32[512,512]{0,1:T(8,128)}, f32[512,512]{0,1:T(8,128)})) %all-reduce.11.cloned.1.call-update) | async-done | bytes 2097168 | tf_op jit(solution)/shard_map/psum | solution.py:45
  362.2 1.6 copy.28
  363.7 1.6 gather_fusion.3
  365.4 0.3 copy.29
  365.7 0.0 copy-start.3
  365.7 3.9 fusion.1
  369.6 0.0 copy-done.3
  369.6 3.0 fusion.3
  372.6 0.0 all-reduce.9.cloned.1.call-update
  372.7 97.4 %all-reduce.9.cloned.1.call-done = f32[512,512]{0,1:T(8,128)} async-done(((f32[512,512]{0,1:T(8,128)}), f32[512,512]{0,1:T(8,128)}) %all-reduce.9.cloned.1.call-update) | async-done | bytes 1048592 | tf_op jit(solution)/shard_map/psum | solution.py:9
  470.1 4.6 fusion
  474.7 3.6 copy.32
  (16 shorter events, 0.2 us)
Async XLA Ops:
  6.5 1.5 copy-start.1
  6.5 121.8 %all-reduce.13.cloned.1.call-start = ((), (), s32[]{:S(2)}) async-start(), calls=%async_computation.3 | async-start | bytes 4194304 | tf_op jit(solution)/shard_map/psum | solution.py:45
  6.5 2.9 copy-start.5
  13.1 225.7 %all-reduce.7.cloned.1.call-start = ((), (), s32[]{:S(2)}) async-start(), calls=%async_computation | async-start | bytes 2097152 | tf_op jit(solution)/shard_map/psum | solution.py:9
  132.2 1.7 copy-start.4
  133.9 4.4 copy-start.2
  137.3 1.0 copy-start
  141.3 220.8 %all-reduce.11.cloned.1.call-start = ((), (), s32[]{:S(2)}) async-start(), calls=%async_computation.2 | async-start | bytes 4194304 | tf_op jit(solution)/shard_map/psum | solution.py:45
  247.4 222.7 %all-reduce.9.cloned.1.call-start = ((), (), s32[]{:S(2)}) async-start(), calls=%async_computation.1 | async-start | bytes 2097152 | tf_op jit(solution)/shard_map/psum | solution.py:9
  365.7 3.9 copy-start.3
Sparse Core Ops, SparseCore 0:
  13.2 115.0 all-reduce.12
  141.5 97.2 all-reduce.6
  247.5 114.6 all-reduce.10
  372.8 97.2 all-reduce.8
where the time goes:
time: 488 us; the launch traced here: 485 us
  waiting for transfers between devices  424 us (87%)
  matrix products  23 us (5%)
  local copies, waits for them, and re-layouts  20.7 us (4%)
  between operations  13.4 us (3%)
    psum x2, waiting for transfers between devices, body(): new_row = lax.psum(picked, 'prow')  229 us
    psum x2, waiting for transfers between devices, spread(): return lax.psum(kept, axis)  195 us
    dot_general x2, matrix products, body(): tile_data = tile_data - jnp.dot(lower_part, upper_part, precision=highest)  9.76 us
  transfers between devices with their start and end apart: 4, of which 4 were waited for; matrix products, arithmetic and copies ran while one was open for 0% of the time, Pallas kernels for 0%

commit v1 on v0

v1 whole, which is shorter than its diff:
```python
import functools

import jax
import jax.numpy as jnp
from jax import lax
from jax.experimental import pallas as pl
from jax.experimental.pallas import tpu as pltpu
from jax.sharding import PartitionSpec as P

MESH = pl.DeviceIdType.MESH
F32 = jnp.float32
BF16 = jnp.bfloat16

N = 512
STEPS = 2
SLOT = 40
HEADS = 2
DEPTH = 640
FIX = 64
PARTS = 3


def dot(a, b):
    return jnp.dot(a, b, preferred_element_type=F32)


def split(v):
    high = v.astype(BF16)
    return high, (v - high.astype(F32)).astype(BF16)


def product(a, b):
    return dot(a[0], b[0]) + (dot(a[0], b[1]) + dot(a[1], b[0]))


def select_rows(chooser, v):
    high = v.astype(BF16)
    rest = v - high.astype(F32)
    mid = rest.astype(BF16)
    low = (rest - mid.astype(F32)).astype(BF16)
    return dot(chooser, high) + (dot(chooser, mid) + dot(chooser, low))


def iota(shape, dim):
    return lax.broadcasted_iota(jnp.int32, shape, dim)


def kernel(
    lin_hbm, piv_ref, linv_hbm, uinv_hbm, out_ref,
    lin, x_ref, li, ui, lsh, lsl, uih, uil, pick, pick_t, slot_row, slot_col,
    pack, f_ref, g_ref, pb, pf, low, upp,
    load_sem, xs, xr, rs, rr, bs, br, ss, sr,
):
    p = lax.axis_index("prow")
    q = lax.axis_index("pcol")
    z, core = p // 2, p % 2
    y, x = q // 4, q % 4
    up_z = lax.rem(z + 1, 8) * 2 + core
    down_z = lax.rem(z + 7, 8) * 2 + core
    sibling = z * 2 + (1 - core)

    def at_x(d):
        return (p, y * 4 + lax.rem(x + d, 4))

    def at_y(d):
        return (p, lax.rem(y + d, 4) * 4 + x)

    barrier = pltpu.get_barrier_semaphore()
    friends = [at_x(1), at_x(2), at_x(3), at_y(1), at_y(2), at_y(3), (up_z, q), (down_z, q), (sibling, q)]
    for friend in friends:
        pl.semaphore_signal(barrier, inc=1, device_id=friend, device_id_type=MESH)

    @pl.when(p >= HEADS)
    def _():
        for head in range(HEADS):
            pl.semaphore_signal(barrier, inc=1, device_id=(head, q), device_id_type=MESH)

    loads = [
        pltpu.make_async_copy(lin_hbm, lin, load_sem.at[0]),
        pltpu.make_async_copy(linv_hbm, li, load_sem.at[1]),
        pltpu.make_async_copy(uinv_hbm, ui, load_sem.at[2]),
    ]
    for load in loads:
        load.start()

    before = (iota((N, N), 0) < iota((N, N), 1)).astype(BF16)
    same = iota((N, N), 0) == iota((N, N), 1)
    first = (p - HEADS) * SLOT
    for s in range(STEPS):
        piv = piv_ref[s : s + 1, :]
        owner = lax.shift_right_logical(piv, 9)
        place = jnp.bitwise_and(piv, N - 1)
        owned = (iota((16, N), 0) == owner).astype(F32)
        rank = jnp.sum(owned * dot(owned.astype(BF16), before), axis=0, keepdims=True)
        slots = ((owner - HEADS) * SLOT).astype(F32) + rank
        slots_down = jnp.sum(jnp.where(same, slots, 0.0), axis=1, keepdims=True)
        place_down = jnp.sum(jnp.where(same, place.astype(F32), 0.0), axis=1, keepdims=True)
        slot_row[s] = slots
        slot_col[s] = slots_down
        mine = (slots == (iota((48, N), 0) + first).astype(F32)).astype(BF16)
        pick[s] = dot(mine, (place_down == iota((N, N), 1).astype(F32)).astype(BF16))[:SLOT]
        across = iota((N, 128), 1)
        mine_t = jnp.logical_and(slots_down == (across + first).astype(F32), across < SLOT)
        pick_t[s] = dot((place.astype(F32) == iota((N, N), 0).astype(F32)).astype(BF16), mine_t.astype(F32).astype(BF16))
        f_ref[s, SLOT:FIX, :] = jnp.zeros((FIX - SLOT, N), F32)
        g_ref[s, 14 * SLOT : DEPTH, :] = jnp.zeros((DEPTH - 14 * SLOT, N), F32)

    loads[0].wait()
    for c in range(4):
        x_ref[:, 128 * c : 128 * (c + 1)] = lin[pl.ds(c, N, stride=4), :]

    @pl.when(p >= HEADS)
    def _():
        pl.semaphore_wait(barrier, len(friends))

    @pl.when(p < HEADS)
    def _():
        pl.semaphore_wait(barrier, len(friends) + 14)

    def remote(src, dst, send, recv, device):
        return pltpu.make_async_remote_copy(
            src_ref=src, dst_ref=dst, send_sem=send, recv_sem=recv, device_id=device, device_id_type=MESH
        )

    def stage(s, carry):
        def rows_of(k, h, i):
            if k < 2:
                return pl.ds(pl.multiple_of(k * 256 + h * 128 + i * 32, 32), 32)
            return pl.ds(pl.multiple_of(h * 32 + i * 8, 8), 8)

        def target(k):
            return pb.at[s] if k < 2 else pf.at[s]

        def source(k):
            return x_ref if k < 2 else f_ref.at[s]

        root = q == s

        def send_index(st, k, h, d):
            return ((st * PARTS + k) * 2 + h) * 3 + d - 1

        def recv_index(st, k, h, d):
            return s * 54 + send_index(st, k, h, d)

        def xy_copy(st, k, h, d):
            if h == 0:
                along_x = st != 1
            else:
                along_x = st == 1
            device = at_x(d) if along_x else at_y(d)
            if st == 0:
                i = lax.rem(x + d, 4) if h == 0 else lax.rem(y + d, 4)
                src = source(k).at[rows_of(k, h, i)]
            else:
                i = x if h == 0 else y
                src = target(k).at[rows_of(k, h, i)]
            dst = target(k).at[rows_of(k, h, i)]
            arrival = d if st == 2 else 1
            return remote(src, dst, xs.at[send_index(st, k, h, d)], xr.at[recv_index(st, k, h, arrival)], device)

        def senders(st, h):
            if st == 0:
                return root
            if st == 1:
                return y == 0 if h == 0 else x == s
            return None

        def receivers(st, h):
            if st == 0:
                return jnp.logical_and(y == 0, x != s) if h == 0 else jnp.logical_and(x == s, y != 0)
            if st == 1:
                return y != 0 if h == 0 else x != s
            return None

        def when(condition, action):
            if condition is None:
                action()
            else:
                pl.when(condition)(action)

        def xy_send(st, k):
            for h in range(2):

                def go(h=h):
                    for d in (1, 2, 3):
                        xy_copy(st, k, h, d).start()

                when(senders(st, h), go)

        def xy_arrive(st, k):
            for h in range(2):

                def go(h=h):
                    for d in (1, 2, 3) if st == 2 else (1,):
                        xy_copy(st, k, h, d).wait_recv()

                when(receivers(st, h), go)

        def xy_sent(st, k):
            for h in range(2):

                def go(h=h):
                    for d in (1, 2, 3):
                        xy_copy(st, k, h, d).wait_send()

                when(senders(st, h), go)

        def xy_keep(k):
            def go():
                for h, i in ((0, x), (1, y)):
                    rows = rows_of(k, h, i)
                    target(k)[rows, :] = source(k)[rows, :]

            pl.when(root)(go)

        def block(zb, lo=0, size=SLOT, c=core):
            return g_ref.at[s, pl.ds(pl.multiple_of((2 * zb + c - HEADS) * SLOT + lo, 8), size)]

        def part(t, side):
            return (0, SLOT) if t < 4 else ((0, 24) if side == 0 else (24, 16))

        def chip(t, side):
            return lax.rem(z + (8 - t if side == 0 else t), 8)

        def ring_copy(t, side, back):
            ref = block(chip(back, side), *part(t, side))
            n = side * 4 + t - 1
            return remote(ref, ref, rs.at[n], rr.at[s * 8 + n], (up_z if side == 0 else down_z, q))

        def core_copy(t, side, c=core):
            ref = block(chip(t, side), *part(t, side), c=c)
            n = 0 if t == 0 else 1 + side * 4 + t - 1
            return remote(ref, ref, bs.at[n], br.at[s * 9 + n], (sibling, q))

        def ring_arrive(t):
            for side in range(2):

                def go(side=side):
                    ring_copy(t, side, t).wait_recv()
                    if t < 4:
                        ring_copy(t + 1, side, t).start()
                    core_copy(t, side).start()

                pl.when(chip(t, side) != 0)(go)

        def scatter_copy(o):
            rows = pl.ds(pl.multiple_of(o * SLOT, 8), SLOT)
            return remote(pack.at[rows], f_ref.at[s, pl.ds(0, SLOT)], ss.at[o], sr.at[s], (o + HEADS, q))

        @pl.when(p == s)
        def _():
            chooser = (slot_row[s] == iota((14 * SLOT, N), 0).astype(F32)).astype(F32).astype(BF16)
            pack[...] = select_rows(chooser, x_ref[...])
            lax.fori_loop(0, 14, lambda o, c: (scatter_copy(o).start(), c)[1], 0)

        @pl.when(z != 0)
        def _():
            g_ref[s, pl.ds(pl.multiple_of((p - HEADS) * SLOT, 8), SLOT), :] = select_rows(
                pick[s].astype(BF16), x_ref[...]
            )
            ring_copy(1, 0, 0).start()
            ring_copy(1, 1, 0).start()
            core_copy(0, 0).start()

        xy_send(0, 0)
        xy_send(0, 1)
        xy_keep(0)
        xy_keep(1)

        @pl.when(s == 0)
        def _():
            loads[1].wait()
            loads[2].wait()

        order = (slot_col[s] == iota((N, DEPTH), 1).astype(F32)).astype(F32).astype(BF16)
        lower = split(li[s])
        lsh[...] = dot(lower[0], order).astype(BF16)
        lsl[...] = dot(lower[1], order).astype(BF16)
        uih[...], uil[...] = split(ui[s])

        ring_arrive(1)
        xy_arrive(0, 0)
        xy_send(1, 0)
        xy_arrive(0, 1)
        xy_send(1, 1)
        ring_arrive(2)

        @pl.when(p >= HEADS)
        def _():
            scatter_copy(0).wait_recv()

        @pl.when(p < HEADS)
        def _():
            f_ref[s, 0:SLOT, :] = jnp.zeros((SLOT, N), F32)

        xy_send(0, 2)
        xy_keep(2)
        xy_arrive(1, 0)
        xy_send(2, 0)
        xy_arrive(0, 2)
        xy_send(1, 2)
        xy_arrive(1, 1)
        xy_send(2, 1)
        ring_arrive(3)
        xy_arrive(1, 2)
        xy_send(2, 2)
        upper_inv = (uih[...], uil[...])
        xy_arrive(2, 0)
        low[0:256, :] = product(split(pb[s, 0:256, :]), upper_inv)
        ring_arrive(4)
        xy_arrive(2, 1)
        low[256:512, :] = product(split(pb[s, 256:512, :]), upper_inv)
        xy_arrive(2, 2)

        chosen_t = pick_t[s].astype(BF16)[:, 0:FIX]
        is_target = jnp.sum(pick_t[s], axis=1, keepdims=True) > 0.5

        @pl.when(p > s)
        def _():
            fixed = product(split(pf[s]), upper_inv)
            low[...] = jnp.where(is_target, select_rows(chosen_t, fixed), low[...])

        for k in range(PARTS):
            for st in range(3):
                xy_sent(st, k)

        @pl.when(p == s)
        def _():
            lax.fori_loop(0, 14, lambda o, c: (scatter_copy(o).wait_send(), c)[1], 0)

        @pl.when(p > s)
        def _():
            x_ref[...] = jnp.where(is_target, select_rows(chosen_t, f_ref[s]), x_ref[...])

        @pl.when(z != 0)
        def _():
            core_copy(0, 0, 1 - core).wait_recv()
            core_copy(0, 0).wait_send()

        for side in range(2):
            for t in (1, 2, 3, 4):

                def arrived(side=side, t=t):
                    core_copy(t, side, 1 - core).wait_recv()
                    core_copy(t, side).wait_send()

                def sent(side=side, t=t):
                    ring_copy(t, side, t - 1).wait_send()

                pl.when(chip(t, side) != 0)(arrived)
                pl.when(chip(t - 1, side) != 0)(sent)

        @pl.when(q > s)
        def _():
            upp[...] = product((lsh[...], lsl[...]), split(g_ref[s]))

        @pl.when(jnp.logical_and(p == s, q <= s))
        def _():
            place = (slot_col[s] == iota((N, DEPTH), 1).astype(F32)).astype(F32).astype(BF16)
            x_ref[...] = select_rows(place, g_ref[s])

        @pl.when(jnp.logical_and(p == s, q > s))
        def _():
            x_ref[...] = upp[...]

        @pl.when(jnp.logical_and(p > s, q == s))
        def _():
            x_ref[...] = low[...]

        @pl.when(jnp.logical_and(p > s, q > s))
        def _():
            x_ref[...] = x_ref[...] - product(split(low[...]), split(upp[...]))

        return carry

    lax.fori_loop(0, STEPS, stage, 0)
    for c in range(4):
        out_ref[pl.ds(c, N, stride=4), :] = x_ref[:, 128 * c : 128 * (c + 1)]


def body(matrix, pivots, lower_inv, upper_inv):
    vm, dma = pltpu.VMEM, pltpu.SemaphoreType.DMA
    any_space = pl.BlockSpec(memory_space=pl.ANY)
    done = pl.pallas_call(
        kernel,
        out_shape=jax.ShapeDtypeStruct((4 * N, 128), F32),
        in_specs=[any_space, pl.BlockSpec(memory_space=vm), any_space, any_space],
        out_specs=pl.BlockSpec(memory_space=vm),
        scratch_shapes=[
            vm((4 * N, 128), F32),
            vm((N, N), F32),
            vm((STEPS, N, N), F32),
            vm((STEPS, N, N), F32),
            vm((N, DEPTH), BF16),
            vm((N, DEPTH), BF16),
            vm((N, N), BF16),
            vm((N, N), BF16),
            vm((STEPS, SLOT, N), F32),
            vm((STEPS, N, 128), F32),
            vm((STEPS, 1, N), F32),
            vm((STEPS, N, 1), F32),
            vm((14 * SLOT, N), F32),
            vm((STEPS, FIX, N), F32),
            vm((STEPS, DEPTH, N), F32),
            vm((STEPS, N, N), F32),
            vm((STEPS, FIX, N), F32),
            vm((N, N), F32),
            vm((N, N), F32),
            dma((3,)),
            dma((54,)),
            dma((108,)),
            dma((8,)),
            dma((16,)),
            dma((9,)),
            dma((18,)),
            dma((14,)),
            dma((STEPS,)),
        ],
        compiler_params=pltpu.CompilerParams(
            collective_id=0, has_side_effects=True, vmem_limit_bytes=56 << 20
        ),
        cost_estimate=pl.CostEstimate(flops=10**10, bytes_accessed=7 << 20, transcendentals=0),
    )(matrix.reshape(4 * N, 128), pivots, lower_inv, upper_inv)
    return done.reshape(matrix.shape)


def solution(mesh):
    placed = (P(None, "prow", None, "pcol"), P(), P(), P())
    return jax.shard_map(
        body, mesh=mesh, in_specs=placed, out_specs=P(None, "prow", None, "pcol"), check_vma=False
    )
```

time: 488 us -> 66.8 us (0.14)
  the two profiles are of different devices: /device:TPU:39 before, /device:TPU:102 now
where the time goes in v1:
time: 66.8 us; the launch traced here: 66.6 us
  Pallas kernels  63.7 us (95%)
  local copies, waits for them, and re-layouts  2.91 us (4%)
    pallas_call x1, Pallas kernels, body(): pl.pallas_call(kernel, out_shape=jax.ShapeDtypeStruct((4 * N, 128), F32),...  63.7 us
    unnamed x1, local copies, waits for them, and re-layouts  2.91 us

profile of v1, /device:TPU:102, one launch (start us, length us, event | category | flops | bytes accessed | tf_op | source)
XLA Modules:
  0.0 66.6 jit_solution(13738031773101936533)
XLA Ops:
  0.0 63.7 %shard_map.46 = f32[2048,128]{1,0:T(8,128)} custom-call(f32[2048,128]{1,0:T(8,128)} %bitcast.3, s32[2,512]{1,0:T(2,128)} %piv_ref.1, f32[2,512,512]{2,1,0:T(8,128)} %linv_hbm.1, f32[2,512,512]{2,1,0:T(8,128)} %uinv_hbm.1), custom_call_target="tpu_custom_call" | custom-call | flops 10000000000 | bytes 7340032 | tf_op jit(solution)/shard_map/pallas_call | solution.py:384
  63.7 2.9 %copy.7 = f32[1,512,1,512]{3,2,1,0:T(1,128)} copy(f32[1,512,1,512]{3,2,1,0:T(1,128)} %bitcast.2) | data formatting | bytes 2097152

commit v2 on v1

v2 whole, which is shorter than its diff:
```python
import functools

import jax
import jax.numpy as jnp
from jax import lax
from jax.experimental import pallas as pl
from jax.experimental.pallas import tpu as pltpu
from jax.sharding import PartitionSpec as P

MESH = pl.DeviceIdType.MESH
F32 = jnp.float32
BF16 = jnp.bfloat16

N = 512
STEPS = 2
SLOT = 40
HEADS = 2
DEPTH = 640
FIX = 48
SIZES = (24, 24, 24, 16, 8)
CHUNKS = len(SIZES) - 1
LONG = 6 * sum(SIZES[:-1])
CUT = 6 * sum(SIZES[:2])
SUB = ((0, 24), (24, 16))
FAR = (6, 7, 4, 5, 8, 9, 2, 3, 10, 11, 0, 1, 12, 13)


def dot(a, b):
    return jnp.dot(a, b, preferred_element_type=F32)


def split(v):
    high = v.astype(BF16)
    return high, (v - high.astype(F32)).astype(BF16)


def product(a, b):
    return dot(a[0], b[0]) + (dot(a[0], b[1]) + dot(a[1], b[0]))


def select_rows(chooser, v):
    high = v.astype(BF16)
    rest = v - high.astype(F32)
    mid = rest.astype(BF16)
    low = (rest - mid.astype(F32)).astype(BF16)
    return dot(chooser, high) + (dot(chooser, mid) + dot(chooser, low))


def iota(shape, dim):
    return lax.broadcasted_iota(jnp.int32, shape, dim)


def kernel(
    lin_hbm, piv_ref, linv_hbm, uinv_hbm, out_ref,
    lin, x_ref, li, ui, lsh, lsl, uih, uil, pick, pick_t, slot_row, slot_col,
    pack, f_ref, g_ref, pb, pf, low, upp,
    load_sem, xs, xr, rs, rr, bs, br, ss, sr,
):
    p = lax.axis_index("prow")
    q = lax.axis_index("pcol")
    z, core = p // 2, p % 2
    y, x = q // 4, q % 4
    along_z = [lax.rem(z + d, 8) * 2 + core for d in (1, 7, 2, 6)]
    sibling = z * 2 + (1 - core)

    def at_x(d):
        return (p, y * 4 + lax.rem(x + d, 4))

    def at_y(d):
        return (p, lax.rem(y + d, 4) * 4 + x)

    barrier = pltpu.get_barrier_semaphore()
    friends = [at_x(1), at_x(2), at_x(3), at_y(1), at_y(2), at_y(3), (sibling, q)]
    friends += [(other, q) for other in along_z]

    @pl.when(p >= HEADS)
    def _():
        for head in range(HEADS):
            pl.semaphore_signal(barrier, inc=1, device_id=(head, q), device_id_type=MESH)

    for friend in friends:
        pl.semaphore_signal(barrier, inc=1, device_id=friend, device_id_type=MESH)

    loads = [
        pltpu.make_async_copy(lin_hbm, lin, load_sem.at[0]),
        pltpu.make_async_copy(linv_hbm, li, load_sem.at[1]),
        pltpu.make_async_copy(uinv_hbm, ui, load_sem.at[2]),
    ]
    for load in loads:
        load.start()

    before = (iota((N, N), 0) < iota((N, N), 1)).astype(BF16)
    same = iota((N, N), 0) == iota((N, N), 1)
    first = (p - HEADS) * SLOT
    empty = jnp.where(z == 0, 0, jnp.where(z < 4, 2 * z - 1, jnp.where(z == 4, 7, 2 * (8 - z))))
    for s in range(STEPS):
        piv = piv_ref[s : s + 1, :]
        owner = lax.shift_right_logical(piv, 9)
        place = jnp.bitwise_and(piv, N - 1)
        owned = (iota((16, N), 0) == owner).astype(F32)
        rank = jnp.sum(owned * dot(owned.astype(BF16), before), axis=0, keepdims=True)
        slots = ((owner - HEADS) * SLOT).astype(F32) + rank
        back = jnp.bitwise_and(z - lax.shift_right_logical(owner, 1), 7)
        turn = jnp.where(back == 0, 0, jnp.where(back < 4, 2 * back - 1, jnp.where(back == 4, 7, 2 * (8 - back))))
        gathered = (turn * (2 * SLOT) + jnp.bitwise_and(owner, 1) * SLOT).astype(F32) + rank
        slots_down = jnp.sum(jnp.where(same, slots, 0.0), axis=1, keepdims=True)
        place_down = jnp.sum(jnp.where(same, place.astype(F32), 0.0), axis=1, keepdims=True)
        slot_row[s] = slots
        slot_col[s] = jnp.sum(jnp.where(same, gathered, 0.0), axis=1, keepdims=True)
        mine = (slots == (iota((48, N), 0) + first).astype(F32)).astype(BF16)
        pick[s] = dot(mine, (place_down == iota((N, N), 1).astype(F32)).astype(BF16))[:SLOT]
        across = iota((N, 128), 1)
        mine_t = jnp.logical_and(slots_down == (across + first).astype(F32), across < SLOT)
        pick_t[s] = dot((place.astype(F32) == iota((N, N), 0).astype(F32)).astype(BF16), mine_t.astype(F32).astype(BF16))
        f_ref[s, SLOT:FIX, :] = jnp.zeros((FIX - SLOT, N), F32)
        g_ref[s, pl.ds(pl.multiple_of(empty * 2 * SLOT, 8), 2 * SLOT), :] = jnp.zeros((2 * SLOT, N), F32)

    x_ref[N:LONG, :] = jnp.zeros((LONG - N, N), F32)
    loads[0].wait()
    for c in range(4):
        x_ref[0:N, 128 * c : 128 * (c + 1)] = lin[pl.ds(c, N, stride=4), :]

    own_rows = pl.ds(pl.multiple_of(core * SLOT, 8), SLOT)

    def choose_own(s):
        @pl.when(z != 0)
        def _():
            g_ref[s, own_rows, :] = select_rows(pick[s].astype(BF16), x_ref[0:N, :])

    def choose_scattered(s):
        @pl.when(p == s)
        def _():
            chooser = (slot_row[s] == iota((14 * SLOT, N), 0).astype(F32)).astype(F32).astype(BF16)
            pack[...] = select_rows(chooser, x_ref[0:N, :])

    choose_own(0)
    choose_scattered(0)

    @pl.when(p >= HEADS)
    def _():
        pl.semaphore_wait(barrier, len(friends))

    @pl.when(p < HEADS)
    def _():
        pl.semaphore_wait(barrier, len(friends) + 14)

    def remote(src, dst, send, recv, device):
        return pltpu.make_async_remote_copy(
            src_ref=src, dst_ref=dst, send_sem=send, recv_sem=recv, device_id=device, device_id_type=MESH
        )

    def stage(s, carry):
        offs = (lax.rem(x - s + 4, 4), y)
        root = q == s

        def rows_of(k, h, d):
            at = 6 * sum(SIZES[:k]) if k < CHUNKS else 0
            return pl.ds(pl.multiple_of(at + (h * 3 + d - 1) * SIZES[k], 8), SIZES[k])

        def target(k):
            return pb.at[s] if k < CHUNKS else pf.at[s]

        def source(k):
            return x_ref if k < CHUNKS else f_ref.at[s]

        def index(st, k, h, d):
            return ((st * (CHUNKS + 1) + k) * 2 + h) * 3 + d - 1

        def xy_copy(st, k, h, d, piece, arrival):
            device = at_x(d) if (h == 0) == (st != 1) else at_y(d)
            rows = rows_of(k, h, piece)
            src = source(k).at[rows] if st == 0 else target(k).at[rows]
            return remote(
                src, target(k).at[rows], xs.at[index(st, k, h, d)],
                xr.at[s * 6 * 3 * (CHUNKS + 1) + index(st, k, h, arrival)], device,
            )

        def each_send(st, k, action):
            for h in range(2):
                mine, other = offs[h], offs[1 - h]
                if st == 0:

                    @pl.when(root)
                    def _(h=h):
                        for d in (1, 2, 3):
                            action(xy_copy(0, k, h, d, d, 1))

                elif st == 1:

                    @pl.when(jnp.logical_and(other == 0, mine != 0))
                    def _(h=h, mine=mine):
                        for d in (1, 2, 3):
                            action(xy_copy(1, k, h, d, mine, 1))

                else:
                    for d in (1, 2, 3):
                        spared = jnp.logical_and(other == 0, lax.rem(mine + d, 4) == 0)

                        @pl.when(jnp.logical_and(mine != 0, jnp.logical_not(spared)))
                        def _(h=h, mine=mine, d=d):
                            action(xy_copy(2, k, h, d, mine, d))

        def xy_send(st, k):
            each_send(st, k, lambda copy: copy.start())

        def xy_sent(st, k):
            each_send(st, k, lambda copy: copy.wait_send())

        def xy_arrive(st, k):
            for h in range(2):
                mine, other = offs[h], offs[1 - h]
                if st == 0:

                    @pl.when(jnp.logical_and(other == 0, mine != 0))
                    def _(h=h, mine=mine):
                        xy_copy(0, k, h, 1, mine, 1).wait_recv()

                elif st == 1:

                    @pl.when(jnp.logical_and(other != 0, mine != 0))
                    def _(h=h, mine=mine):
                        xy_copy(1, k, h, 1, mine, 1).wait_recv()

                else:
                    for d in (1, 2, 3):
                        giver = lax.rem(mine + 4 - d, 4)

                        @pl.when(jnp.logical_and(giver != 0, jnp.logical_not(root)))
                        def _(h=h, d=d, giver=giver):
                            xy_copy(2, k, h, d, giver, d).wait_recv()

        def chip(t, side):
            return lax.rem(z + (8 - t if side == 0 else t), 8)

        def block(t, side, c, part):
            turn = 0 if t == 0 else (7 if t == 4 else 2 * t - 1 + side)
            return g_ref.at[s, pl.ds(pl.multiple_of(turn * 2 * SLOT + c * SLOT + part[0], 8), part[1])]

        def ring_copy(t, side):
            n = side * 4 + t - 1
            part = SUB[side] if t == 4 else (0, SLOT)
            return remote(
                block(0 if t < 3 else 2, side, core, part), block(t, side, core, part),
                rs.at[n], rr.at[s * 8 + n], (along_z[side if t % 2 else 2 + side], q),
            )

        def core_copy(t, side, c=core):
            ref = block(t, side, c, SUB[side] if t == 4 else (0, SLOT))
            n = 0 if t == 0 else 1 + side * 4 + t - 1
            return remote(ref, ref, bs.at[n], br.at[s * 9 + n], (sibling, q))

        def ring_arrive(t):
            for side in range(2):

                @pl.when(chip(t, side) != 0)
                def _(side=side):
                    ring_copy(t, side).wait_recv()
                    if t == 2:
                        ring_copy(3, side).start()
                        ring_copy(4, side).start()
                    core_copy(t, side).start()

        def scatter_copy(o):
            rows = pl.ds(o * SLOT, SLOT)
            return remote(pack.at[rows], f_ref.at[s, pl.ds(0, SLOT)], ss.at[o], sr.at[s], (o + HEADS, q))

        def scatter(owners):
            @pl.when(p == s)
            def _():
                for o in owners:
                    scatter_copy(o).start()

        for k in range(CHUNKS):
            xy_send(0, k)

        @pl.when(s != 0)
        def _():
            choose_own(s)

        @pl.when(z != 0)
        def _():
            for t in (1, 2):
                ring_copy(t, 0).start()
                ring_copy(t, 1).start()
            core_copy(0, 0).start()

        @pl.when(s != 0)
        def _():
            choose_scattered(s)

        scatter(FAR[:8])

        @pl.when(root)
        def _():
            pb[s] = x_ref[...]

        @pl.when(s == 0)
        def _():
            loads[1].wait()
            loads[2].wait()

        order = (slot_col[s] == iota((N, DEPTH), 1).astype(F32)).astype(F32).astype(BF16)
        lower = split(li[s])
        lsh[...] = dot(lower[0], order).astype(BF16)
        lsl[...] = dot(lower[1], order).astype(BF16)
        uih[...], uil[...] = split(ui[s])

        def move(st, k):
            xy_arrive(st, k)
            xy_send(st + 1, k)

        chosen_t = pick_t[s].astype(BF16)[:, 0:FIX]
        is_target = jnp.sum(pick_t[s], axis=1, keepdims=True) > 0.5
        upper_inv = (uih[...], uil[...])
        trailing = q > s

        def from_core(t, side):
            @pl.when(chip(t, side) != 0)
            def _():
                core_copy(t, side, 1 - core).wait_recv()
                core_copy(t, side).wait_send()

        def gather_step(lo, hi, start=False):
            @pl.when(trailing)
            def _():
                term = product((lsh[:, lo:hi], lsl[:, lo:hi]), split(g_ref[s, lo:hi, :]))
                upp[...] = term if start else upp[...] + term

        def multiply(lo, hi):
            low[lo:hi, :] = product(split(pb[s, lo:hi, :]), upper_inv)

        def finish(lo, hi):
            @pl.when(p > s)
            def _():
                fixed = product(split(pf[s]), upper_inv)
                rows = jnp.where(is_target[lo:hi], select_rows(chosen_t[lo:hi], fixed), low[lo:hi, :])

                @pl.when(trailing)
                def _():
                    x_ref[lo:hi, :] = x_ref[lo:hi, :] - product(split(rows), split(upp[...]))

                @pl.when(root)
                def _():
                    x_ref[lo:hi, :] = rows

        move(0, 0)
        move(0, 1)
        scatter(FAR[8:])
        move(0, 2)
        move(1, 0)
        move(0, 3)
        ring_arrive(1)
        ring_arrive(2)
        move(1, 1)
        @pl.when(p >= HEADS)
        def _():
            scatter_copy(0).wait_recv()

        @pl.when(p < HEADS)
        def _():
            f_ref[s, 0:SLOT, :] = jnp.zeros((SLOT, N), F32)

        xy_send(0, CHUNKS)
        move(1, 2)
        move(0, CHUNKS)
        move(1, 3)
        move(1, CHUNKS)

        @pl.when(root)
        def _():
            pf[s] = f_ref[s]

        from_core(0, 0)
        for t in (1, 2):
            for side in range(2):
                from_core(t, side)
        gather_step(0, 256, True)
        xy_arrive(2, 0)
        xy_arrive(2, 1)
        multiply(0, CUT)
        ring_arrive(3)
        ring_arrive(4)
        for k in range(CHUNKS + 1):
            xy_sent(0, k)

        @pl.when(p > s)
        def _():
            x_ref[0:N, :] = jnp.where(is_target, select_rows(chosen_t, f_ref[s]), x_ref[0:N, :])

        for t in (3, 4):
            for side in range(2):
                from_core(t, side)
        gather_step(256, DEPTH)
        xy_arrive(2, 2)
        xy_arrive(2, 3)
        multiply(CUT, LONG)
        xy_arrive(2, CHUNKS)
        finish(0, N)

        @pl.when(jnp.logical_and(p == s, q <= s))
        def _():
            place = (slot_col[s] == iota((N, DEPTH), 1).astype(F32)).astype(F32).astype(BF16)
            x_ref[0:N, :] = select_rows(place, g_ref[s])

        @pl.when(jnp.logical_and(p == s, trailing))
        def _():
            x_ref[0:N, :] = upp[...]

        for k in range(CHUNKS + 1):
            for st in (1, 2):
                xy_sent(st, k)

        @pl.when(p == s)
        def _():
            for o in FAR:
                scatter_copy(o).wait_send()

        for side in range(2):
            for t in (1, 2, 3, 4):

                @pl.when(chip(0 if t < 3 else 2, side) != 0)
                def _(side=side, t=t):
                    ring_copy(t, side).wait_send()

        return carry

    lax.fori_loop(0, STEPS, stage, 0)
    for c in range(4):
        out_ref[pl.ds(c, N, stride=4), :] = x_ref[0:N, 128 * c : 128 * (c + 1)]


def body(matrix, pivots, lower_inv, upper_inv):
    vm, dma = pltpu.VMEM, pltpu.SemaphoreType.DMA
    any_space = pl.BlockSpec(memory_space=pl.ANY)
    done = pl.pallas_call(
        kernel,
        out_shape=jax.ShapeDtypeStruct((4 * N, 128), F32),
        in_specs=[any_space, pl.BlockSpec(memory_space=vm), any_space, any_space],
        out_specs=pl.BlockSpec(memory_space=vm),
        scratch_shapes=[
            vm((4 * N, 128), F32),
            vm((LONG, N), F32),
            vm((STEPS, N, N), F32),
            vm((STEPS, N, N), F32),
            vm((N, DEPTH), BF16),
            vm((N, DEPTH), BF16),
            vm((N, N), BF16),
            vm((N, N), BF16),
            vm((STEPS, SLOT, N), F32),
            vm((STEPS, N, 128), F32),
            vm((STEPS, 1, N), F32),
            vm((STEPS, N, 1), F32),
            vm((14 * SLOT, N), F32),
            vm((STEPS, FIX, N), F32),
            vm((STEPS, DEPTH, N), F32),
            vm((STEPS, LONG, N), F32),
            vm((STEPS, FIX, N), F32),
            vm((LONG, N), F32),
            vm((N, N), F32),
            dma((3,)),
            dma((18 * (CHUNKS + 1),)),
            dma((STEPS * 18 * (CHUNKS + 1),)),
            dma((8,)),
            dma((STEPS * 8,)),
            dma((9,)),
            dma((18,)),
            dma((14,)),
            dma((STEPS,)),
        ],
        compiler_params=pltpu.CompilerParams(
            collective_id=0, has_side_effects=True, vmem_limit_bytes=56 << 20
        ),
        cost_estimate=pl.CostEstimate(flops=10**10, bytes_accessed=7 << 20, transcendentals=0),
    )(matrix.reshape(4 * N, 128), pivots, lower_inv, upper_inv)
    return done.reshape(matrix.shape)


def solution(mesh):
    placed = (P(None, "prow", None, "pcol"), P(), P(), P())
    return jax.shard_map(
        body, mesh=mesh, in_specs=placed, out_specs=P(None, "prow", None, "pcol"), check_vma=False
    )
```

time: 66.8 us -> 60.8 us (0.910)
  the two profiles are of different devices: /device:TPU:102 before, /device:TPU:39 now
where the time goes in v2:
time: 60.8 us; the launch traced here: 60.7 us
  Pallas kernels  57.8 us (95%)
  local copies, waits for them, and re-layouts  2.91 us (5%)
    pallas_call x1, Pallas kernels, body(): pl.pallas_call(kernel, out_shape=jax.ShapeDtypeStruct((4 * N, 128), F32),...  57.8 us
    unnamed x1, local copies, waits for them, and re-layouts  2.91 us

profile of v2, /device:TPU:39, one launch (start us, length us, event | category | flops | bytes accessed | tf_op | source)
XLA Modules:
  0.0 60.7 jit_solution(16792739626067094740)
XLA Ops:
  0.0 57.8 %shard_map.46 = f32[2048,128]{1,0:T(8,128)} custom-call(f32[2048,128]{1,0:T(8,128)} %bitcast.3, s32[2,512]{1,0:T(2,128)} %piv_ref.1, f32[2,512,512]{2,1,0:T(8,128)} %linv_hbm.1, f32[2,512,512]{2,1,0:T(8,128)} %uinv_hbm.1), custom_call_target="tpu_custom_call" | custom-call | flops 10000000000 | bytes 7340032 | tf_op jit(solution)/shard_map/pallas_call | solution.py:435
  57.8 2.9 %copy.7 = f32[1,512,1,512]{3,2,1,0:T(1,128)} copy(f32[1,512,1,512]{3,2,1,0:T(1,128)} %bitcast.2) | data formatting | bytes 2097152

commit v3 on v2

--- a/solution.py
+++ b/solution.py
@@ -151,7 +151,8 @@
 
     def stage(s, carry):
         offs = (lax.rem(x - s + 4, 4), y)
-        root = q == s
+        below = p > s
+        root = jnp.logical_and(q == s, below)
 
         def rows_of(k, h, d):
             at = 6 * sum(SIZES[:k]) if k < CHUNKS else 0
@@ -187,7 +188,7 @@
 
                 elif st == 1:
 
-                    @pl.when(jnp.logical_and(other == 0, mine != 0))
+                    @pl.when(jnp.logical_and(below, jnp.logical_and(other == 0, mine != 0)))
                     def _(h=h, mine=mine):
                         for d in (1, 2, 3):
                             action(xy_copy(1, k, h, d, mine, 1))
@@ -196,7 +197,7 @@
                     for d in (1, 2, 3):
                         spared = jnp.logical_and(other == 0, lax.rem(mine + d, 4) == 0)
 
-                        @pl.when(jnp.logical_and(mine != 0, jnp.logical_not(spared)))
+                        @pl.when(jnp.logical_and(below, jnp.logical_and(mine != 0, jnp.logical_not(spared))))
                         def _(h=h, mine=mine, d=d):
                             action(xy_copy(2, k, h, d, mine, d))
 
@@ -211,13 +212,13 @@
                 mine, other = offs[h], offs[1 - h]
                 if st == 0:
 
-                    @pl.when(jnp.logical_and(other == 0, mine != 0))
+                    @pl.when(jnp.logical_and(below, jnp.logical_and(other == 0, mine != 0)))
                     def _(h=h, mine=mine):
                         xy_copy(0, k, h, 1, mine, 1).wait_recv()
 
                 elif st == 1:
 
-                    @pl.when(jnp.logical_and(other != 0, mine != 0))
+                    @pl.when(jnp.logical_and(below, jnp.logical_and(other != 0, mine != 0)))
                     def _(h=h, mine=mine):
                         xy_copy(1, k, h, 1, mine, 1).wait_recv()
 
@@ -225,7 +226,7 @@
                     for d in (1, 2, 3):
                         giver = lax.rem(mine + 4 - d, 4)
 
-                        @pl.when(jnp.logical_and(giver != 0, jnp.logical_not(root)))
+                        @pl.when(jnp.logical_and(below, jnp.logical_and(giver != 0, jnp.logical_not(root))))
                         def _(h=h, d=d, giver=giver):
                             xy_copy(2, k, h, d, giver, d).wait_recv()
 
@@ -249,15 +250,45 @@
             n = 0 if t == 0 else 1 + side * 4 + t - 1
             return remote(ref, ref, bs.at[n], br.at[s * 9 + n], (sibling, q))
 
+        trailing = q > s
+
+        def either(everywhere, toward):
+            return jnp.logical_or(
+                jnp.logical_and(trailing, everywhere), jnp.logical_and(jnp.logical_not(trailing), toward)
+            )
+
+        def sends(t, side):
+            ahead = lax.rem(8 - z, 8) if side == 0 else z
+            toward = {1: ahead == 1, 2: jnp.logical_and(ahead >= 2, ahead <= 4), 3: ahead == 1, 4: ahead == 2}[t]
+            return either(chip(0 if t < 3 else 2, side) != 0, toward)
+
+        def receives(t, side):
+            ahead = lax.rem(8 - z, 8) if side == 0 else z
+            return either(chip(t, side) != 0, ahead <= 2 if t == 2 else ahead == 0)
+
+        def shares(t, side):
+            if t == 0:
+                return jnp.logical_and(trailing, z != 0)
+            return either(chip(t, side) != 0, z == 0)
+
+        def ring_start(t, side):
+            @pl.when(sends(t, side))
+            def _():
+                ring_copy(t, side).start()
+
         def ring_arrive(t):
             for side in range(2):
 
-                @pl.when(chip(t, side) != 0)
+                @pl.when(receives(t, side))
                 def _(side=side):
                     ring_copy(t, side).wait_recv()
-                    if t == 2:
-                        ring_copy(3, side).start()
-                        ring_copy(4, side).start()
+
+                if t == 2:
+                    ring_start(3, side)
+                    ring_start(4, side)
+
+                @pl.when(shares(t, side))
+                def _(side=side):
                     core_copy(t, side).start()
 
         def scatter_copy(o):
@@ -277,11 +308,12 @@
         def _():
             choose_own(s)
 
-        @pl.when(z != 0)
-        def _():
-            for t in (1, 2):
-                ring_copy(t, 0).start()
-                ring_copy(t, 1).start()
+        for t in (1, 2):
+            for side in range(2):
+                ring_start(t, side)
+
+        @pl.when(shares(0, 0))
+        def _():
             core_copy(0, 0).start()
 
         @pl.when(s != 0)
@@ -312,10 +344,9 @@
         chosen_t = pick_t[s].astype(BF16)[:, 0:FIX]
         is_target = jnp.sum(pick_t[s], axis=1, keepdims=True) > 0.5
         upper_inv = (uih[...], uil[...])
-        trailing = q > s
 
         def from_core(t, side):
-            @pl.when(chip(t, side) != 0)
+            @pl.when(shares(t, side))
             def _():
                 core_copy(t, side, 1 - core).wait_recv()
                 core_copy(t, side).wait_send()
@@ -327,42 +358,56 @@
                 upp[...] = term if start else upp[...] + term
 
         def multiply(lo, hi):
-            low[lo:hi, :] = product(split(pb[s, lo:hi, :]), upper_inv)
+            @pl.when(below)
+            def _():
+                low[lo:hi, :] = product(split(pb[s, lo:hi, :]), upper_inv)
 
         def finish(lo, hi):
-            @pl.when(p > s)
+            @pl.when(jnp.logical_and(below, trailing))
+            def _():
+                x_ref[lo:hi, :] = x_ref[lo:hi, :] - product(split(low[lo:hi, :]), split(upp[...]))
+
+            @pl.when(root)
+            def _():
+                x_ref[lo:hi, :] = low[lo:hi, :]
+
+        def swap_in():
+            @pl.when(jnp.logical_and(below, q >= s))
             def _():
                 fixed = product(split(pf[s]), upper_inv)
-                rows = jnp.where(is_target[lo:hi], select_rows(chosen_t[lo:hi], fixed), low[lo:hi, :])
+
+                @pl.when(root)
+                def _():
+                    f_ref[s] = fixed
 
                 @pl.when(trailing)
                 def _():
-                    x_ref[lo:hi, :] = x_ref[lo:hi, :] - product(split(rows), split(upp[...]))
-
-                @pl.when(root)
-                def _():
-                    x_ref[lo:hi, :] = rows
-
+                    f_ref[s] = f_ref[s] - product(split(fixed), split(upp[...]))
+
+            @pl.when(below)
+            def _():
+                x_ref[0:N, :] = jnp.where(is_target, select_rows(chosen_t, f_ref[s]), x_ref[0:N, :])
+
+        scatter(FAR[8:])
         move(0, 0)
         move(0, 1)
-        scatter(FAR[8:])
         move(0, 2)
         move(1, 0)
         move(0, 3)
         ring_arrive(1)
         ring_arrive(2)
+        @pl.when(p < HEADS)
+        def _():
+            f_ref[s, 0:SLOT, :] = jnp.zeros((SLOT, N), F32)
+
+        @pl.when(jnp.logical_and(p >= HEADS, root))
+        def _():
+            scatter_copy(0).wait_recv()
+
+        xy_send(0, CHUNKS)
         move(1, 1)
-        @pl.when(p >= HEADS)
-        def _():
-            scatter_copy(0).wait_recv()
-
-        @pl.when(p < HEADS)
-        def _():
-            f_ref[s, 0:SLOT, :] = jnp.zeros((SLOT, N), F32)
-
-        xy_send(0, CHUNKS)
+        move(0, CHUNKS)
         move(1, 2)
-        move(0, CHUNKS)
         move(1, 3)
         move(1, CHUNKS)
 
@@ -383,19 +428,22 @@
         for k in range(CHUNKS + 1):
             xy_sent(0, k)
 
-        @pl.when(p > s)
-        def _():
-            x_ref[0:N, :] = jnp.where(is_target, select_rows(chosen_t, f_ref[s]), x_ref[0:N, :])
-
         for t in (3, 4):
             for side in range(2):
                 from_core(t, side)
         gather_step(256, DEPTH)
+        finish(0, CUT)
         xy_arrive(2, 2)
         xy_arrive(2, 3)
         multiply(CUT, LONG)
+        finish(CUT, N)
         xy_arrive(2, CHUNKS)
-        finish(0, N)
+
+        @pl.when(jnp.logical_and(p >= HEADS, jnp.logical_not(root)))
+        def _():
+            scatter_copy(0).wait_recv()
+
+        swap_in()
 
         @pl.when(jnp.logical_and(p == s, q <= s))
         def _():
@@ -418,7 +466,7 @@
         for side in range(2):
             for t in (1, 2, 3, 4):
 
-                @pl.when(chip(0 if t < 3 else 2, side) != 0)
+                @pl.when(sends(t, side))
                 def _(side=side, t=t):
                     ring_copy(t, side).wait_send()
 

time: 60.8 us -> 57.8 us (0.951)
  Pallas kernels: 57.8 us -> 54.7 us
    pallas_call x1, Pallas kernels: 57.8 us -> 54.7 us  [body(): pl.pallas_call(kernel, out_shape=jax.ShapeDtypeStruct((4 * N, 128), F32),...]
where the time goes in v3:
time: 57.8 us; the launch traced here: 57.6 us
  Pallas kernels  54.7 us (95%)
  local copies, waits for them, and re-layouts  2.91 us (5%)
    pallas_call x1, Pallas kernels, body(): pl.pallas_call(kernel, out_shape=jax.ShapeDtypeStruct((4 * N, 128), F32),...  54.7 us
    unnamed x1, local copies, waits for them, and re-layouts  2.91 us

profile of v3, /device:TPU:39, one launch (start us, length us, event | category | flops | bytes accessed | tf_op | source)
XLA Modules:
  0.0 57.6 jit_solution(8745387906539579952)
XLA Ops:
  0.0 54.7 %shard_map.46 = f32[2048,128]{1,0:T(8,128)} custom-call(f32[2048,128]{1,0:T(8,128)} %bitcast.3, s32[2,512]{1,0:T(2,128)} %piv_ref.1, f32[2,512,512]{2,1,0:T(8,128)} %linv_hbm.1, f32[2,512,512]{2,1,0:T(8,128)} %uinv_hbm.1), custom_call_target="tpu_custom_call" | custom-call | flops 10000000000 | bytes 7340032 | tf_op jit(solution)/shard_map/pallas_call | solution.py:483
  54.7 2.9 %copy.7 = f32[1,512,1,512]{3,2,1,0:T(1,128)} copy(f32[1,512,1,512]{3,2,1,0:T(1,128)} %bitcast.2) | data formatting | bytes 2097152

commit v4 on v3

--- a/solution.py
+++ b/solution.py
@@ -308,7 +308,7 @@
         def _():
             choose_own(s)
 
-        for t in (1, 2):
+        for t in (2, 1):
             for side in range(2):
                 ring_start(t, side)
 
@@ -394,8 +394,8 @@
         move(0, 2)
         move(1, 0)
         move(0, 3)
+        ring_arrive(2)
         ring_arrive(1)
-        ring_arrive(2)
         @pl.when(p < HEADS)
         def _():
             f_ref[s, 0:SLOT, :] = jnp.zeros((SLOT, N), F32)

time: 57.8 us -> 57.8 us (level)
  no operation moved by 1% of the time
where the time goes in v4:
time: 57.8 us; the launch traced here: 57.6 us
  Pallas kernels  54.7 us (95%)
  local copies, waits for them, and re-layouts  2.91 us (5%)
    pallas_call x1, Pallas kernels, body(): pl.pallas_call(kernel, out_shape=jax.ShapeDtypeStruct((4 * N, 128), F32),...  54.7 us
    unnamed x1, local copies, waits for them, and re-layouts  2.91 us

profile of v4, /device:TPU:39, one launch (start us, length us, event | category | flops | bytes accessed | tf_op | source)
XLA Modules:
  0.0 57.6 jit_solution(7210333448033789630)
XLA Ops:
  0.0 54.7 %shard_map.46 = f32[2048,128]{1,0:T(8,128)} custom-call(f32[2048,128]{1,0:T(8,128)} %bitcast.3, s32[2,512]{1,0:T(2,128)} %piv_ref.1, f32[2,512,512]{2,1,0:T(8,128)} %linv_hbm.1, f32[2,512,512]{2,1,0:T(8,128)} %uinv_hbm.1), custom_call_target="tpu_custom_call" | custom-call | flops 10000000000 | bytes 7340032 | tf_op jit(solution)/shard_map/pallas_call | solution.py:483
  54.7 2.9 %copy.7 = f32[1,512,1,512]{3,2,1,0:T(1,128)} copy(f32[1,512,1,512]{3,2,1,0:T(1,128)} %bitcast.2) | data formatting | bytes 2097152
